TPU v7x, 32 devices: a whole 2x2x4 slice. The times are simulated.
32 devices in a mesh: grp: 2 (over x), tile: 16 (over z, y, core).
Axes of the slice: x: 2, y: 2, z: 4, core: 2. Of those that a mesh axis runs over, the one named last changes fastest.
Arguments:
- features: bfloat16 [768, 48, 48, 128], P(('grp', 'tile')), parts along dimension 0, may hold values from -6 to 6
- edge_table: int32 [384, 4, 2], replicated, may hold values from 0 to 383, as said below
- w_enc0: bfloat16 [3, 3, 128, 128], replicated, may hold values from -0.25 to 0.25
- w_enc1: bfloat16 [3, 3, 128, 128], replicated, may hold values from -0.25 to 0.25
- w_enc2: bfloat16 [3, 3, 128, 128], replicated, may hold values from -0.25 to 0.25
- w_mid: bfloat16 [3, 3, 128, 128], replicated, may hold values from -0.25 to 0.25
- w_dec2: bfloat16 [3, 3, 256, 128], replicated, may hold values from -0.1875 to 0.1875
- w_dec1: bfloat16 [3, 3, 256, 128], replicated, may hold values from -0.1875 to 0.1875
- w_dec0: bfloat16 [3, 3, 256, 128], replicated, may hold values from -0.1875 to 0.1875
Outputs:
- decoded: bfloat16 [768, 48, 48, 128], P(('grp', 'tile')), parts along dimension 0
There are 2 independent parts, one for each index of `grp`. A program takes and returns all parts, laid end to end along the dimension named above; an argument that names none is the same for every part. Nothing has to cross between parts.
Inputs may be any that keep to these rules, and one draw needn't show every extreme that they name: `edge_table`: edges are numbered 0 for row 0, 1 for the last column, 2 for the last row, 3 for column 0 of a tile; pairs are symmetric, with the same reversal flag on both sides. The tiles are those of a cube with 8 x 8 tiles a face, numbered face by face (faces +x, -x, +y, -y, +z, -z; on the face of axis k, rows run along axis k+1 and columns along axis k+2, modulo 3) and row by row within a face; blocks of 24 consecutive tiles of that numbering are placed on the devices in an order drawn at random, and the arrays hold the tiles in device order.
All inputs are finite; a program needn't handle non-finite values.
Results may differ from a plain program's by a relative error of at most 0.0053.
Values may be sent and summed in bfloat16 or wider, within the bound.
No kernel may reach another device: no remote copies, remote signals or barrier semaphores. Data moves between devices by JAX's collectives and lax.ppermute only.
A program may use at most 128 MiB of HBM per device.

v0:
```python
import jax
import jax.numpy as jnp
import numpy as np
from jax import lax
from jax.sharding import PartitionSpec as P

FACE_TILES = 8


def shortened(array):
    return jax.tree.map(lambda a: a.astype(jnp.bfloat16) if a.dtype == jnp.float32 else a, array)


def cube_links(tiles_side):
    basis = np.eye(3, dtype=np.int64)
    frames = []
    for axis_id in range(3):
        for orient in (1, -1):
            frames.append(
                (orient * basis[axis_id], basis[(axis_id + 1) % 3], basis[(axis_id + 2) % 3])
            )
    per_face = tiles_side * tiles_side
    tile_total = 6 * per_face
    centres = np.zeros((tile_total, 3), np.int64)
    lookup = {}
    for face_id in range(6):
        normal, row_axis, col_axis = frames[face_id]
        for row_id in range(tiles_side):
            for col_id in range(tiles_side):
                slot_id = face_id * per_face + row_id * tiles_side + col_id
                centre = (
                    tiles_side * normal
                    + (2 * row_id + 1 - tiles_side) * row_axis
                    + (2 * col_id + 1 - tiles_side) * col_axis
                )
                centres[slot_id] = centre
                lookup[tuple((int(entry) for entry in centre))] = slot_id
    partner = np.zeros((tile_total, 4), np.int64)
    for slot_id in range(tile_total):
        normal, row_axis, col_axis = frames[slot_id // per_face]
        outward = (-row_axis, col_axis, row_axis, -col_axis)
        for edge_id in range(4):
            beyond = tuple((int(entry) for entry in centres[slot_id] + 2 * outward[edge_id]))
            if beyond in lookup:
                partner[slot_id, edge_id] = lookup[beyond]
            else:
                partner[slot_id, edge_id] = lookup[
                    tuple((int(entry) for entry in centres[slot_id] + outward[edge_id] - normal))
                ]
    return partner


def pair_capacity(tiles_side, tiles_here):
    partner = cube_links(tiles_side)
    tile_total = partner.shape[0]
    blocks = tile_total // tiles_here
    source = np.repeat(np.arange(tile_total) // tiles_here, 4)
    target = partner.reshape(-1) // tiles_here
    identity = np.eye(blocks, dtype=np.int64)
    shared = identity[source].T @ identity[target]
    shared = shared * (1 - identity)
    return max(int(shared.max()), 1)


def routing_plan(edge_table, position, tiles_here, slot_count, devices):
    strip_count = tiles_here * 4
    own_rows = lax.dynamic_slice_in_dim(edge_table, position * tiles_here, tiles_here, 0).reshape(
        strip_count, 2
    )
    partner = own_rows[:, 0]
    matching = own_rows[:, 1] // 2
    reversed_rows = own_rows[:, 1] % 2 == 1
    target = partner // tiles_here
    order = jnp.arange(strip_count, dtype=jnp.int32)
    earlier = (order[None, :] < order[:, None]) & (target[None, :] == target[:, None])
    slot_rank = jnp.sum(earlier.astype(jnp.int32), axis=1)
    remote = target != position
    slot_row = target * slot_count + slot_rank
    buffer_rows = jnp.arange(devices * slot_count, dtype=jnp.int32)
    send_map = ((slot_row[None, :] == buffer_rows[:, None]) & remote[None, :]).astype(jnp.bfloat16)
    source_tiles = target[:, None] * tiles_here + jnp.arange(tiles_here, dtype=jnp.int32)[None, :]
    their_partners = jnp.take(edge_table[:, :, 0], source_tiles, axis=0).reshape(
        strip_count, strip_count
    )
    toward_me = their_partners // tiles_here == position
    wanted = partner % tiles_here * 4 + matching
    before_wanted = order[None, :] < wanted[:, None]
    recv_rank = jnp.sum((toward_me & before_wanted).astype(jnp.int32), axis=1)
    pick_row = jnp.where(remote, target * slot_count + recv_rank, devices * slot_count + wanted)
    pick_columns = jnp.arange(devices * slot_count + strip_count, dtype=jnp.int32)
    pick_map = (pick_row[:, None] == pick_columns[None, :]).astype(jnp.bfloat16)
    return (send_map, pick_map, reversed_rows)


def edge_rims(field):
    return jnp.stack([field[:, 0], field[:, :, -1], field[:, -1], field[:, :, 0]], axis=1)


def assemble(field, halo_rows):
    upper_side = halo_rows[:, 0]
    right_side = halo_rows[:, 1]
    lower_side = halo_rows[:, 2]
    left_side = halo_rows[:, 3]

    def corner(one_side, other_side):
        return ((one_side.astype(jnp.float32) + other_side.astype(jnp.float32)) * 0.5).astype(
            field.dtype
        )[:, None]

    upper_row = jnp.concatenate(
        [
            corner(upper_side[:, 0], left_side[:, 0]),
            upper_side,
            corner(upper_side[:, -1], right_side[:, 0]),
        ],
        axis=1,
    )
    lower_row = jnp.concatenate(
        [
            corner(lower_side[:, 0], left_side[:, -1]),
            lower_side,
            corner(lower_side[:, -1], right_side[:, -1]),
        ],
        axis=1,
    )
    middle_rows = jnp.concatenate([left_side[:, :, None], field, right_side[:, :, None]], axis=2)
    return jnp.concatenate([upper_row[:, None], middle_rows, lower_row[:, None]], axis=1)


def conv_layer(padded, weight):
    summed = lax.conv_general_dilated(
        padded,
        weight,
        (1, 1),
        "VALID",
        dimension_numbers=("NHWC", "HWIO", "NHWC"),
        preferred_element_type=jnp.float32,
    )
    return jax.nn.silu(summed).astype(jnp.bfloat16)


def shrink(field):
    count, length, _, channels = field.shape
    blocks = field.astype(jnp.float32).reshape(count, length // 2, 2, length // 2, 2, channels)
    return (jnp.sum(blocks, axis=(2, 4)) * 0.25).astype(jnp.bfloat16)


def enlarge(field):
    return jnp.repeat(jnp.repeat(field, 2, axis=1), 2, axis=2)


def trade_main(outgoing):
    return jax.tree.map(
        lambda part, own: part.astype(own.dtype),
        lax.all_to_all(shortened(outgoing), "tile", split_axis=0, concat_axis=0, tiled=True),
        outgoing,
    )


def trade_coarse(outgoing):
    return jax.tree.map(
        lambda part, own: part.astype(own.dtype),
        lax.all_to_all(shortened(outgoing), "tile", split_axis=0, concat_axis=0, tiled=True),
        outgoing,
    )


def trade_skip(outgoing):
    return jax.tree.map(
        lambda part, own: part.astype(own.dtype),
        lax.all_to_all(shortened(outgoing), "tile", split_axis=0, concat_axis=0, tiled=True),
        outgoing,
    )


def per_device(features, edge_table, w_enc0, w_enc1, w_enc2, w_mid, w_dec2, w_dec1, w_dec0):
    tiles_here = features.shape[0]
    devices = lax.axis_size("tile")
    position = lax.axis_index("tile")
    slot_count = pair_capacity(FACE_TILES, tiles_here)
    send_map, pick_map, reversed_rows = routing_plan(
        edge_table, position, tiles_here, slot_count, devices
    )

    def reverse_some(strips):
        return jnp.where(reversed_rows[:, None, None], strips[:, ::-1, :], strips)

    def halo_of(field, exchanger):
        strips = edge_rims(field)
        strip_count = tiles_here * 4
        length = strips.shape[2]
        channels = strips.shape[3]
        strips = strips.reshape(strip_count, length, channels)
        flattened = strips.reshape(strip_count, length * channels)
        outgoing = jnp.dot(send_map, flattened, preferred_element_type=jnp.float32).astype(
            jnp.bfloat16
        )
        incoming = exchanger(outgoing.reshape(devices, slot_count, length * channels))
        gathered = jnp.concatenate(
            [incoming.reshape(devices * slot_count, length * channels), flattened], axis=0
        )
        halo_rows = jnp.dot(pick_map, gathered, preferred_element_type=jnp.float32).astype(
            jnp.bfloat16
        )
        halo_rows = halo_rows.reshape(strip_count, length, channels)
        halo_rows = reverse_some(halo_rows)
        return halo_rows.reshape(tiles_here, 4, length, channels)

    encoders = (w_enc0, w_enc1, w_enc2)
    decoders = (w_dec0, w_dec1, w_dec2)
    current = features
    skip_fields = []
    skip_halos = []
    for level_id in range(3):
        current = conv_layer(assemble(current, halo_of(current, trade_main)), encoders[level_id])
        skip_fields.append(current)
        skip_halos.append(halo_of(current, trade_skip))
        current = shrink(current)
    current = conv_layer(assemble(current, halo_of(current, trade_main)), w_mid)
    for level_id in (2, 1, 0):
        skip_field = skip_fields[level_id]
        coarse_halo = halo_of(current, trade_coarse)
        upper_part = assemble(enlarge(current), jnp.repeat(coarse_halo, 2, axis=2))
        lower_part = assemble(skip_field, skip_halos[level_id])
        padded = jnp.concatenate([upper_part, lower_part], axis=3)
        current = conv_layer(padded, decoders[level_id])
    return current


def solution(mesh):
    return jax.shard_map(
        per_device,
        mesh=mesh,
        in_specs=(P(("grp", "tile"), None, None, None), P(), P(), P(), P(), P(), P(), P(), P()),
        out_specs=P(("grp", "tile"), None, None, None),
        check_vma=False,
    )
```

profile of v0, /device:TPU:15, one launch (start us, length us, event | category | flops | bytes accessed | tf_op | source)
XLA Modules:
  0.0 603.4 jit_solution(13620522086932720696)
XLA Ops:
  1.2 1.8 fusion.230
  3.0 3.3 fusion.231
  6.6 3.9 gather_fusion
  12.4 2.1 convolution_convert_fusion.1
  14.5 3.4 reshape.317
  17.9 6.5 %all-to-all-start = ((bf16[16,11,6144]{2,1,0:T(8,128)(2,1)}), bf16[16,11,6144]{2,1,0:T(8,128)(2,1)}, u32[]{:S(2)}, u32[]{:S(2)}) async-start(bf16[16,11,6144]{2,1,0:T(8,128)(2,1)} %reshape.317), calls=%async_computation | async-start | bytes 6291456 | tf_op jit(solution)/shard_map/all_to_all | solution.py:155
  25.8 15.2 %copy.292 = bf16[24,48,48,128]{3,0,2,1:T(8,128)(2,1)} copy(bf16[24,48,48,128]{3,2,1,0:T(8,128)(2,1)} %param.9) | data formatting | bytes 28311552 | tf_op args[0]
  41.1 53.3 %all-to-all-done = bf16[16,11,6144]{2,1,0:T(8,128)(2,1)} async-done(((bf16[16,11,6144]{2,1,0:T(8,128)(2,1)}), bf16[16,11,6144]{2,1,0:T(8,128)(2,1)}, u32[]{:S(2)}, u32[]{:S(2)}) %all-to-all-start) | async-done | bytes 2162720 | tf_op jit(solution)/shard_map/all_to_all | solution.py:155
  94.4 2.3 reshape.318
  96.7 2.3 fusion.103
  99.3 3.4 rev.30
  104.0 40.4 %multiply_convert_fusion.1 = bf16[24,48,48,128]{3,0,2,1:T(8,128)(2,1)S(1)} fusion(bf16[3,3,128,128]{3,2,1,0:T(8,128)(2,1)S(1)} %copy-done.40, bf16[24,1,50,128]{3,0,2,1:T(8,128)(2,1)S(1)} %maximum_bitcast_fusion.1, bf16[24,48,1,128]{3,0,2,1:T(8,128)(2,1)S(1)} %bitcast.512, bf16[24,48,48,128]{3,0,2,1:T(8,128)(2,1)} %copy.292, ...), kind=kOutput, calls=%fused_computation.23 | convolution fusion | flops 16373563392 | bytes 29810688 | tf_op jit(solution)/shard_map/conv_general_dilated | solution.py:131
  144.4 3.3 convert_reduce_fusion
  147.7 2.0 copy-done.2
  150.6 1.7 copy-done.9
  154.4 5.1 all-to-all-start.1
  160.4 35.3 %all-to-all-done.1 = bf16[16,11,3072]{2,1,0:T(8,128)(2,1)S(1)} async-done(((bf16[16,11,3072]{2,1,0:T(8,128)(2,1)}), bf16[16,11,3072]{2,1,0:T(8,128)(2,1)S(1)}, u32[]{:S(2)}, u32[]{:S(2)}) %all-to-all-start.1) | async-done | bytes 1081376 | tf_op jit(solution)/shard_map/all_to_all | solution.py:155
  196.1 1.7 fusion.109
  197.9 2.1 rev.31
  202.0 9.7 %multiply_convert_fusion.3 = bf16[24,24,24,128]{3,0,2,1:T(8,128)(2,1)S(1)} fusion(bf16[3,3,128,128]{3,2,1,0:T(8,128)(2,1)S(1)} %copy-done.41, bf16[24,1,26,128]{3,0,2,1:T(8,128)(2,1)S(1)} %maximum_bitcast_fusion.7, bf16[24,24,1,128]{3,0,2,1:T(8,128)(2,1)S(1)} %bitcast.524, bf16[24,24,24,128]{3,0,2,1:T(8,128)(2,1)S(1)} %copy-done.10, ...), kind=kOutput, calls=%fused_computation.58 | convolution fusion | flops 4094017536 | bytes 7987200 | tf_op jit(solution)/shard_map/conv_general_dilated | solution.py:131
  215.3 5.4 all-to-all-start.2
  223.3 2.1 convolution_convert_fusion
  225.5 3.3 reshape.368
  228.8 1.8 slice_bitcast_fusion.11
  230.6 9.3 %all-to-all-done.2 = bf16[16,11,1536]{2,1,0:T(8,128)(2,1)S(1)} async-done(((bf16[16,11,1536]{2,1,0:T(8,128)(2,1)}), bf16[16,11,1536]{2,1,0:T(8,128)(2,1)S(1)}, u32[]{:S(2)}, u32[]{:S(2)}) %all-to-all-start.2) | async-done | bytes 540704 | tf_op jit(solution)/shard_map/all_to_all | solution.py:155
  240.9 1.5 convolution_convert_fusion.15
  244.2 2.5 multiply_convert_fusion.6
  249.4 5.1 all-to-all-start.3
  257.8 7.5 %all-to-all-done.3 = bf16[16,11,768]{2,1,0:T(8,128)(2,1)S(1)} async-done(((bf16[16,11,768]{2,1,0:T(8,128)(2,1)}), bf16[16,11,768]{2,1,0:T(8,128)(2,1)S(1)}, u32[]{:S(2)}, u32[]{:S(2)}) %all-to-all-start.3) | async-done | bytes 270368 | tf_op jit(solution)/shard_map/all_to_all | solution.py:155
  265.3 5.6 all-to-all-start.5
  275.9 14.3 %all-to-all-done.5 = bf16[16,11,1536]{2,1,0:T(8,128)(2,1)} async-done(((bf16[16,11,1536]{2,1,0:T(8,128)(2,1)}), bf16[16,11,1536]{2,1,0:T(8,128)(2,1)}, u32[]{:S(2)}, u32[]{:S(2)}) %all-to-all-start.5) | async-done | bytes 540704 | tf_op jit(solution)/shard_map/all_to_all | solution.py:171
  290.2 5.2 all-to-all-start.7
  295.7 1.9 multiply_convert_fusion.8
  299.2 1.8 reshape.339
  301.0 2.1 reshape.347
  303.2 2.3 convolution_convert_fusion.14
  305.4 1.9 reshape.348
  307.4 2.0 rev.35
  311.4 20.0 %all-to-all-done.7 = bf16[16,11,3072]{2,1,0:T(8,128)(2,1)S(1)} async-done(((bf16[16,11,3072]{2,1,0:T(8,128)(2,1)}), bf16[16,11,3072]{2,1,0:T(8,128)(2,1)S(1)}, u32[]{:S(2)}, u32[]{:S(2)}) %all-to-all-start.7) | async-done | bytes 1081376 | tf_op jit(solution)/shard_map/all_to_all | solution.py:171
  331.5 4.9 all-to-all-start.4
  336.4 2.2 fusion.242
  343.3 1.6 maximum_bitcast_fusion.16
  344.9 1.5 maximum_bitcast_fusion.17
  347.2 1.8 reshape.340
  351.8 5.3 multiply_convert_fusion.5
  359.4 5.3 all-to-all-start.6
  364.6 2.0 fusion.112
  366.8 2.3 rev.37
  371.9 12.0 %all-to-all-done.6 = bf16[16,11,1536]{2,1,0:T(8,128)(2,1)S(1)} async-done(((bf16[16,11,1536]{2,1,0:T(8,128)(2,1)}), bf16[16,11,1536]{2,1,0:T(8,128)(2,1)S(1)}, u32[]{:S(2)}, u32[]{:S(2)}) %all-to-all-start.6) | async-done | bytes 540704 | tf_op jit(solution)/shard_map/all_to_all | solution.py:163
  383.9 5.3 all-to-all-start.9
  395.4 17.2 %multiply_convert_fusion.2 = bf16[24,24,24,128]{3,0,2,1:T(8,128)(2,1)S(1)} fusion(bf16[3,3,256,128]{3,2,1,0:T(8,128)(2,1)S(1)} %copy-done.39, bf16[24,1,26,128]{3,0,2,1:T(8,128)(2,1)S(1)} %copy-done.34, bf16[24,24,1,128]{3,0,2,1:T(8,128)(2,1)S(1)} %bitcast.520, bf16[24,24,24,128]{3,0,2,1:T(8,128)(2,1)S(1)} %copy-done.6, ...), kind=kOutput, calls=%fused_computation.57 | convolution fusion | flops 8245641216 | bytes 12435456 | tf_op jit(solution)/shard_map/conv_general_dilated | solution.py:131
  412.7 1.7 copy-done.7
  417.2 41.9 %all-to-all-done.9 = bf16[16,11,6144]{2,1,0:T(8,128)(2,1)} async-done(((bf16[16,11,6144]{2,1,0:T(8,128)(2,1)}), bf16[16,11,6144]{2,1,0:T(8,128)(2,1)}, u32[]{:S(2)}, u32[]{:S(2)}) %all-to-all-start.9) | async-done | bytes 2162720 | tf_op jit(solution)/shard_map/all_to_all | solution.py:171
  459.0 5.2 all-to-all-start.8
  465.6 3.4 reshape.369
  469.1 2.6 fusion.106
  471.9 3.4 rev.39
  479.7 20.6 %all-to-all-done.8 = bf16[16,11,3072]{2,1,0:T(8,128)(2,1)S(1)} async-done(((bf16[16,11,3072]{2,1,0:T(8,128)(2,1)}), bf16[16,11,3072]{2,1,0:T(8,128)(2,1)S(1)}, u32[]{:S(2)}, u32[]{:S(2)}) %all-to-all-start.8) | async-done | bytes 1081376 | tf_op jit(solution)/shard_map/all_to_all | solution.py:163
  500.8 1.7 fusion.115
  502.6 2.1 rev.38
  506.9 1.9 broadcast_in_dim.240
  508.9 6.2 %broadcast_in_dim.241 = bf16[24,48,24,2,128]{4,0,3,2,1:T(8,128)(2,1)} broadcast(bf16[24,48,24,128]{3,0,2,1:T(8,128)(2,1)S(1)} %bitcast.425), dimensions={0,1,2,4} | broadcast | bytes 21233664 | tf_op jit(solution)/shard_map/broadcast_in_dim | solution.py:149
  515.1 73.8 %multiply_convert_fusion = bf16[24,48,48,128]{3,0,2,1:T(8,128)(2,1)} fusion(bf16[3,3,256,128]{3,2,1,0:T(8,128)(2,1)S(1)} %copy-done, bf16[24,1,50,128]{3,0,2,1:T(8,128)(2,1)S(1)} %copy-done.28, bf16[24,48,1,128]{3,0,2,1:T(8,128)(2,1)S(1)} %bitcast.508, bf16[24,48,48,128]{3,0,2,1:T(8,128)(2,1)} %copy-done.2, bf16[24,48,1,128]{3,0,2,1:T(8,128)(2,1)S(1)} %bitcast.510, ...), kind=kOutput, calls=%fused_computation.22 | convolution fusion | flops 32957497344 | bytes 45465600 | tf_op jit(solution)/shard_map/conv_general_dilated | solution.py:131
  588.9 14.0 %copy.361 = bf16[24,48,48,128]{3,2,1,0:T(8,128)(2,1)} copy(bf16[24,48,48,128]{3,0,2,1:T(8,128)(2,1)} %multiply_convert_fusion) | data formatting | bytes 28311552 | tf_op jit(solution)/shard_map/convert_element_type | solution.py:139
  (280 shorter events, 66.8 us)
Async XLA Ops:
  0.0 515.1 %copy-start = (bf16[3,3,256,128]{3,2,1,0:T(8,128)(2,1)S(1)}, bf16[3,3,256,128]{3,2,1,0:T(8,128)(2,1)}, u32[]{:S(2)}) copy-start(bf16[3,3,256,128]{3,2,1,0:T(8,128)(2,1)} %param.17) | copy-start | bytes 1769476
  0.0 6.4 %slice-start = ((s32[384,4,2]{0,2,1:T(2,128)}), s32[384,4,1]{0,2,1:T(1,128)S(1)}, s32[]{:S(2)}) async-start(s32[384,4,2]{0,2,1:T(2,128)} %param.10), calls=%async_computation.10 | async-start | bytes 12288 | tf_op jit(solution)/shard_map/slice | solution.py:82
  17.9 76.5 %all-to-all-start = ((bf16[16,11,6144]{2,1,0:T(8,128)(2,1)}), bf16[16,11,6144]{2,1,0:T(8,128)(2,1)}, u32[]{:S(2)}, u32[]{:S(2)}) async-start(bf16[16,11,6144]{2,1,0:T(8,128)(2,1)} %reshape.317), calls=%async_computation | async-start | bytes 6291456 | tf_op jit(solution)/shard_map/all_to_all | solution.py:155
  103.1 1.0 copy-start.40
  144.4 5.3 copy-start.2
  150.6 1.8 copy-start.9
  154.4 41.3 %all-to-all-start.1 = ((bf16[16,11,3072]{2,1,0:T(8,128)(2,1)}), bf16[16,11,3072]{2,1,0:T(8,128)(2,1)S(1)}, u32[]{:S(2)}, u32[]{:S(2)}) async-start(bf16[16,11,3072]{2,1,0:T(8,128)(2,1)} %reshape.323), calls=%async_computation.1 | async-start | bytes 3145728 | tf_op jit(solution)/shard_map/all_to_all | solution.py:155
  197.8 2.7 copy-start.41
  200.0 2.0 copy-start.10
  211.8 1.8 copy-start.5
  213.9 9.1 %copy-start.17 = (bf16[12,8,12,128]{3,1,2,0:T(8,128)(2,1)}, bf16[12,8,12,128]{3,1,2,0:T(8,128)(2,1)S(1)}, u32[]{:S(2)}) copy-start(bf16[12,8,12,128]{3,1,2,0:T(8,128)(2,1)S(1)} %copy.485) | copy-start | bytes 884740
  215.3 24.6 %all-to-all-start.2 = ((bf16[16,11,1536]{2,1,0:T(8,128)(2,1)}), bf16[16,11,1536]{2,1,0:T(8,128)(2,1)S(1)}, u32[]{:S(2)}, u32[]{:S(2)}) async-start(bf16[16,11,1536]{2,1,0:T(8,128)(2,1)} %reshape.329), calls=%async_computation.2 | async-start | bytes 1572864 | tf_op jit(solution)/shard_map/all_to_all | solution.py:155
  243.2 1.0 copy-start.42
  246.7 9.0 %copy-start.11 = (bf16[24,12,12,128]{3,0,2,1:T(8,128)(2,1)}, bf16[24,12,12,128]{3,0,2,1:T(8,128)(2,1)S(1)}, u32[]{:S(2)}) copy-start(bf16[24,12,12,128]{3,0,2,1:T(8,128)(2,1)S(1)} %multiply_convert_fusion.6) | copy-start | bytes 2654212
  247.6 0.7 copy-start.20
  249.4 22.4 %copy-start.21 = (bf16[24,1,24,128]{3,0,2,1:T(8,128)(2,1)S(1)}, bf16[24,1,24,128]{3,0,2,1:T(8,128)(2,1)}, u32[]{:S(2)}) copy-start(bf16[24,1,24,128]{3,0,2,1:T(8,128)(2,1)} %get-tuple-element.24) | copy-start | bytes 442372
  249.4 22.4 %copy-start.22 = (bf16[24,1,24,128]{3,0,2,1:T(8,128)(2,1)S(1)}, bf16[24,1,24,128]{3,0,2,1:T(8,128)(2,1)}, u32[]{:S(2)}) copy-start(bf16[24,1,24,128]{3,0,2,1:T(8,128)(2,1)} %get-tuple-element.25) | copy-start | bytes 442372
  249.4 15.8 %all-to-all-start.3 = ((bf16[16,11,768]{2,1,0:T(8,128)(2,1)}), bf16[16,11,768]{2,1,0:T(8,128)(2,1)S(1)}, u32[]{:S(2)}, u32[]{:S(2)}) async-start(bf16[16,11,768]{2,1,0:T(8,128)(2,1)} %reshape.335), calls=%async_computation.3 | async-start | bytes 786432 | tf_op jit(solution)/shard_map/all_to_all | solution.py:155
  255.7 0.7 copy-start.16
  265.3 24.9 %all-to-all-start.5 = ((bf16[16,11,1536]{2,1,0:T(8,128)(2,1)}), bf16[16,11,1536]{2,1,0:T(8,128)(2,1)}, u32[]{:S(2)}, u32[]{:S(2)}) async-start(bf16[16,11,1536]{2,1,0:T(8,128)(2,1)} %reshape.346), calls=%async_computation.5 | async-start | bytes 1572864 | tf_op jit(solution)/shard_map/all_to_all | solution.py:171
  290.2 41.3 %all-to-all-start.7 = ((bf16[16,11,3072]{2,1,0:T(8,128)(2,1)}), bf16[16,11,3072]{2,1,0:T(8,128)(2,1)S(1)}, u32[]{:S(2)}, u32[]{:S(2)}) async-start(bf16[16,11,3072]{2,1,0:T(8,128)(2,1)} %reshape.357), calls=%async_computation.7 | async-start | bytes 3145728 | tf_op jit(solution)/shard_map/all_to_all | solution.py:171
  297.6 0.7 copy-start.18
  331.5 15.8 %all-to-all-start.4 = ((bf16[16,11,768]{2,1,0:T(8,128)(2,1)}), bf16[16,11,768]{2,1,0:T(8,128)(2,1)}, u32[]{:S(2)}, u32[]{:S(2)}) async-start(bf16[16,11,768]{2,1,0:T(8,128)(2,1)} %reshape.339), calls=%async_computation.4 | async-start | bytes 786432 | tf_op jit(solution)/shard_map/all_to_all | solution.py:163
  342.4 8.7 %copy-start.19 = (bf16[24,6,6,128]{3,0,2,1:T(8,128)(2,1)S(1)}, bf16[24,6,6,128]{3,0,2,1:T(8,128)(2,1)}, u32[]{:S(2)}) copy-start(bf16[24,6,6,128]{3,0,2,1:T(8,128)(2,1)} %copy-done.18) | copy-start | bytes 663556
  343.3 8.1 %copy-start.12 = (bf16[24,12,12,128]{3,0,2,1:T(8,128)(2,1)S(1)}, bf16[24,12,12,128]{3,0,2,1:T(8,128)(2,1)}, u32[]{:S(2)}) copy-start(bf16[24,12,12,128]{3,0,2,1:T(8,128)(2,1)} %copy-done.11) | copy-start | bytes 2654212
  343.3 8.1 %copy-start.35 = (bf16[24,1,12,128]{3,0,2,1:T(8,128)(2,1)S(1)}, bf16[24,1,12,128]{3,0,2,1:T(8,128)(2,1)}, u32[]{:S(2)}) copy-start(bf16[24,1,12,128]{3,0,2,1:T(8,128)(2,1)} %copy.510) | copy-start | bytes 221188
  350.3 1.1 copy-start.36
  350.3 1.1 copy-start.37
  350.7 1.1 copy-start.38
  357.1 0.9 copy-start.13
  359.4 24.5 %all-to-all-start.6 = ((bf16[16,11,1536]{2,1,0:T(8,128)(2,1)}), bf16[16,11,1536]{2,1,0:T(8,128)(2,1)S(1)}, u32[]{:S(2)}, u32[]{:S(2)}) async-start(bf16[16,11,1536]{2,1,0:T(8,128)(2,1)} %reshape.350), calls=%async_computation.6 | async-start | bytes 1572864 | tf_op jit(solution)/shard_map/all_to_all | solution.py:163
  370.4 0.8 copy-start.29
  370.4 13.4 %copy-start.31 = (bf16[24,1,24,128]{3,0,2,1:T(8,128)(2,1)}, bf16[24,1,24,128]{3,0,2,1:T(8,128)(2,1)S(1)}, u32[]{:S(2)}) copy-start(bf16[24,1,24,128]{3,0,2,1:T(8,128)(2,1)S(1)} %copy.501) | copy-start | bytes 442372
  383.9 75.2 %all-to-all-start.9 = ((bf16[16,11,6144]{2,1,0:T(8,128)(2,1)}), bf16[16,11,6144]{2,1,0:T(8,128)(2,1)}, u32[]{:S(2)}, u32[]{:S(2)}) async-start(bf16[16,11,6144]{2,1,0:T(8,128)(2,1)} %reshape.368), calls=%async_computation.9 | async-start | bytes 6291456 | tf_op jit(solution)/shard_map/all_to_all | solution.py:171
  390.5 2.5 copy-start.14
  393.1 2.0 copy-start.6
  393.1 2.0 copy-start.30
  393.1 2.0 copy-start.32
  393.1 2.0 copy-start.33
  393.1 2.1 copy-start.34
  393.1 2.3 copy-start.39
  412.6 1.8 copy-start.7
  414.6 0.8 copy-start.3
  459.0 41.3 %all-to-all-start.8 = ((bf16[16,11,3072]{2,1,0:T(8,128)(2,1)}), bf16[16,11,3072]{2,1,0:T(8,128)(2,1)S(1)}, u32[]{:S(2)}, u32[]{:S(2)}) async-start(bf16[16,11,3072]{2,1,0:T(8,128)(2,1)} %reshape.361), calls=%async_computation.8 | async-start | bytes 3145728 | tf_op jit(solution)/shard_map/all_to_all | solution.py:163
  465.6 3.4 copy-start.15
  476.8 2.0 copy-start.4
  477.0 1.0 copy-start.23
  477.1 0.9 copy-start.25
  504.9 2.0 copy-start.8
  508.8 6.3 %copy-start.24 = (bf16[24,1,48,128]{3,0,2,1:T(8,128)(2,1)S(1)}, bf16[24,1,48,128]{3,0,2,1:T(8,128)(2,1)}, u32[]{:S(2)}) copy-start(bf16[24,1,48,128]{3,0,2,1:T(8,128)(2,1)} %copy-done.23) | copy-start | bytes 884740
  508.8 6.3 %copy-start.26 = (bf16[24,1,48,128]{3,0,2,1:T(8,128)(2,1)S(1)}, bf16[24,1,48,128]{3,0,2,1:T(8,128)(2,1)}, u32[]{:S(2)}) copy-start(bf16[24,1,48,128]{3,0,2,1:T(8,128)(2,1)} %copy-done.25) | copy-start | bytes 884740
  508.8 6.2 %copy-start.27 = (bf16[24,1,50,128]{3,0,2,1:T(8,128)(2,1)S(1)}, bf16[24,1,50,128]{3,0,2,1:T(8,128)(2,1)}, u32[]{:S(2)}) copy-start(bf16[24,1,50,128]{3,0,2,1:T(8,128)(2,1)} %maximum_bitcast_fusion.4) | copy-start | bytes 921604
  508.9 6.2 %copy-start.28 = (bf16[24,1,50,128]{3,0,2,1:T(8,128)(2,1)S(1)}, bf16[24,1,50,128]{3,0,2,1:T(8,128)(2,1)}, u32[]{:S(2)}) copy-start(bf16[24,1,50,128]{3,0,2,1:T(8,128)(2,1)} %maximum_bitcast_fusion.5) | copy-start | bytes 921604
  588.9 14.0 %copy-start.1 = (bf16[3,3,256,128]{3,2,1,0:T(8,128)(2,1)S(1)}, bf16[3,3,256,128]{3,2,1,0:T(8,128)(2,1)}, u32[]{:S(2)}) copy-start(bf16[3,3,256,128]{3,2,1,0:T(8,128)(2,1)} %param.17) | copy-start | bytes 1769476
where the time goes:
time: 611 us; the launch traced here: 603 us
  waiting for transfers between devices  215 us (35%)
  matrix products  175 us (29%)
  local copies, waits for them, and re-layouts  137 us (22%)
  starting transfers between devices  53.6 us (9%)
  other arithmetic  20.7 us (3%)
    conv_general_dilated x7, matrix products, conv_layer(): lax.conv_general_dilated(padded, weight, (1, 1), 'VALID', dimension_numbe...  151 us
    all_to_all x4, waiting for transfers between devices, trade_main(): lax.all_to_all(shortened(outgoing), 'tile', split_axis=0, concat_axis=0,...  105 us
    all_to_all x3, waiting for transfers between devices, trade_skip(): lax.all_to_all(shortened(outgoing), 'tile', split_axis=0, concat_axis=0,...  76.2 us
    unnamed x131, local copies, waits for them, and re-layouts  40.3 us
    all_to_all x3, waiting for transfers between devices, trade_coarse(): lax.all_to_all(shortened(outgoing), 'tile', split_axis=0, concat_axis=0,...  33.4 us
    all_to_all x4, starting transfers between devices, trade_main(): lax.all_to_all(shortened(outgoing), 'tile', split_axis=0, concat_axis=0,...  22.1 us
    reshape x10, local copies, waits for them, and re-layouts, halo_of(): outgoing.reshape(devices, slot_count, length * channels)  16.9 us
    rev x10, local copies, waits for them, and re-layouts, reverse_some(): return jnp.where(reversed_rows[:, None, None], strips[:, ::-1, :], strips)  16.8 us
  transfers between devices with their start and end apart: 10, of which 10 were waited for; matrix products, arithmetic and copies ran while one was open for 18% of the time, Pallas kernels for 0%

commit v1 on v0

v1 whole, which is shorter than its diff:
```python
import jax
import jax.numpy as jnp
import numpy as np
from jax import lax
from jax.experimental import pallas as pl
from jax.experimental.pallas import tpu as pltpu
from jax.sharding import PartitionSpec as P

FACE_TILES = 8
VMEM_LIMIT = 50 * 2**20
BF = jnp.bfloat16
F32 = jnp.float32


def cube_links(tiles_side):
    basis = np.eye(3, dtype=np.int64)
    frames = []
    for axis_id in range(3):
        for orient in (1, -1):
            frames.append(
                (orient * basis[axis_id], basis[(axis_id + 1) % 3], basis[(axis_id + 2) % 3])
            )
    per_face = tiles_side * tiles_side
    tile_total = 6 * per_face
    centres = np.zeros((tile_total, 3), np.int64)
    lookup = {}
    for face_id in range(6):
        normal, row_axis, col_axis = frames[face_id]
        for row_id in range(tiles_side):
            for col_id in range(tiles_side):
                slot_id = face_id * per_face + row_id * tiles_side + col_id
                centre = (
                    tiles_side * normal
                    + (2 * row_id + 1 - tiles_side) * row_axis
                    + (2 * col_id + 1 - tiles_side) * col_axis
                )
                centres[slot_id] = centre
                lookup[tuple((int(entry) for entry in centre))] = slot_id
    partner = np.zeros((tile_total, 4), np.int64)
    for slot_id in range(tile_total):
        normal, row_axis, col_axis = frames[slot_id // per_face]
        outward = (-row_axis, col_axis, row_axis, -col_axis)
        for edge_id in range(4):
            beyond = tuple((int(entry) for entry in centres[slot_id] + 2 * outward[edge_id]))
            if beyond in lookup:
                partner[slot_id, edge_id] = lookup[beyond]
            else:
                partner[slot_id, edge_id] = lookup[
                    tuple((int(entry) for entry in centres[slot_id] + outward[edge_id] - normal))
                ]
    return partner


def pair_capacity(tiles_side, tiles_here):
    partner = cube_links(tiles_side)
    tile_total = partner.shape[0]
    blocks = tile_total // tiles_here
    source = np.repeat(np.arange(tile_total) // tiles_here, 4)
    target = partner.reshape(-1) // tiles_here
    identity = np.eye(blocks, dtype=np.int64)
    shared = identity[source].T @ identity[target]
    shared = shared * (1 - identity)
    return max(int(shared.max()), 1)


def routing_plan(edge_table, position, tiles_here, slot_count, devices):
    strip_count = tiles_here * 4
    own_rows = lax.dynamic_slice_in_dim(edge_table, position * tiles_here, tiles_here, 0).reshape(
        strip_count, 2
    )
    partner = own_rows[:, 0]
    matching = own_rows[:, 1] // 2
    reversed_rows = own_rows[:, 1] % 2
    target = partner // tiles_here
    order = jnp.arange(strip_count, dtype=jnp.int32)
    earlier = (order[None, :] < order[:, None]) & (target[None, :] == target[:, None])
    slot_rank = jnp.sum(earlier.astype(jnp.int32), axis=1)
    remote = target != position
    slot_row = jnp.where(remote, target * slot_count + slot_rank, -1)
    source_tiles = target[:, None] * tiles_here + jnp.arange(tiles_here, dtype=jnp.int32)[None, :]
    their_partners = jnp.take(edge_table[:, :, 0], source_tiles, axis=0).reshape(
        strip_count, strip_count
    )
    toward_me = their_partners // tiles_here == position
    wanted = partner % tiles_here * 4 + matching
    before_wanted = order[None, :] < wanted[:, None]
    recv_rank = jnp.sum((toward_me & before_wanted).astype(jnp.int32), axis=1)
    pick_row = jnp.where(remote, target * slot_count + recv_rank, devices * slot_count + wanted)
    return (slot_row, pick_row, reversed_rows)


def edge_rims(field):
    return jnp.stack([field[:, 0], field[:, :, -1], field[:, -1], field[:, :, 0]], axis=1)


def assemble(field, halo_rows):
    upper_side = halo_rows[:, 0]
    right_side = halo_rows[:, 1]
    lower_side = halo_rows[:, 2]
    left_side = halo_rows[:, 3]

    def corner(one_side, other_side):
        return ((one_side.astype(F32) + other_side.astype(F32)) * 0.5).astype(field.dtype)[:, None]

    upper_row = jnp.concatenate(
        [
            corner(upper_side[:, 0], left_side[:, 0]),
            upper_side,
            corner(upper_side[:, -1], right_side[:, 0]),
        ],
        axis=1,
    )
    lower_row = jnp.concatenate(
        [
            corner(lower_side[:, 0], left_side[:, -1]),
            lower_side,
            corner(lower_side[:, -1], right_side[:, -1]),
        ],
        axis=1,
    )
    middle_rows = jnp.concatenate([left_side[:, :, None], field, right_side[:, :, None]], axis=2)
    return jnp.concatenate([upper_row[:, None], middle_rows, lower_row[:, None]], axis=1)


def conv_layer(padded, weight):
    summed = lax.conv_general_dilated(
        padded,
        weight,
        (1, 1),
        "VALID",
        dimension_numbers=("NHWC", "HWIO", "NHWC"),
        preferred_element_type=F32,
    )
    return jax.nn.silu(summed).astype(BF)


def shrink(field):
    count, length, _, channels = field.shape
    blocks = field.astype(F32).reshape(count, length // 2, 2, length // 2, 2, channels)
    return (jnp.sum(blocks, axis=(2, 4)) * 0.25).astype(BF)


def enlarge(field):
    return jnp.repeat(jnp.repeat(field, 2, axis=1), 2, axis=2)


def up16(n):
    return (n + 15) // 16 * 16


def params():
    return pltpu.CompilerParams(vmem_limit_bytes=VMEM_LIMIT)


def column_strips(read_cols, n, colbuf):
    colbuf[...] = read_cols(0).reshape(n * 8, 128)
    left = colbuf[pl.ds(0, n, 8), :]
    colbuf[...] = read_cols(n - 8).reshape(n * 8, 128)
    right = colbuf[pl.ds(7, n, 8), :]
    return left, right


def rims_kernel(x_ref, out_ref, colbuf):
    n = x_ref.shape[1]
    left, right = column_strips(lambda lo: x_ref[0, :, lo : lo + 8, :].astype(F32), n, colbuf)
    out_ref[0, 0] = x_ref[0, 0]
    out_ref[0, 1] = right.astype(BF)
    out_ref[0, 2] = x_ref[0, n - 1]
    out_ref[0, 3] = left.astype(BF)


def tile_rims(x):
    tiles, n, _, c = x.shape
    return pl.pallas_call(
        rims_kernel,
        grid=(tiles,),
        in_specs=[pl.BlockSpec((1, n, n, c), lambda i: (i, 0, 0, 0))],
        out_specs=pl.BlockSpec((1, 4, n, c), lambda i: (i, 0, 0, 0)),
        out_shape=jax.ShapeDtypeStruct((tiles, 4, n, c), BF),
        scratch_shapes=[pltpu.VMEM((n * 8, 128), F32)],
        compiler_params=params(),
        name="tile_rims",
    )(x)


def pack_kernel(slot_ref, rims_ref, send_ref):
    def step(i, carry):
        slot = slot_ref[i]

        @pl.when(slot >= 0)
        def _():
            send_ref[slot] = rims_ref[i]

        return carry

    lax.fori_loop(0, rims_ref.shape[0], step, 0)


def pack_strips(slot_row, rims, rows):
    strips, length, c = rims.shape
    return pl.pallas_call(
        pack_kernel,
        in_specs=[
            pl.BlockSpec(memory_space=pltpu.SMEM),
            pl.BlockSpec(memory_space=pltpu.VMEM),
        ],
        out_specs=pl.BlockSpec(memory_space=pltpu.VMEM),
        out_shape=jax.ShapeDtypeStruct((rows, length, c), BF),
        compiler_params=params(),
        name="pack_strips",
    )(slot_row, rims)


def route_kernel(pick_ref, rev_ref, recv_ref, own_ref, out_ref):
    rows = recv_ref.shape[0]
    length = recv_ref.shape[1]
    ri = lax.broadcasted_iota(jnp.int32, (length, length), 0)
    ci = lax.broadcasted_iota(jnp.int32, (length, length), 1)
    flip = (ri + ci == length - 1).astype(F32).astype(BF)

    def step(i, carry):
        pick = pick_ref[i]

        @pl.when(pick < rows)
        def _():
            out_ref[i] = recv_ref[jnp.minimum(pick, rows - 1)]

        @pl.when(pick >= rows)
        def _():
            out_ref[i] = own_ref[jnp.maximum(pick - rows, 0)]

        @pl.when(rev_ref[i] == 1)
        def _():
            out_ref[i] = jnp.dot(flip, out_ref[i], preferred_element_type=F32).astype(BF)

        return carry

    lax.fori_loop(0, out_ref.shape[0], step, 0)


def route_strips(pick_row, rev, recv, own):
    strips, length, c = own.shape
    smem = pl.BlockSpec(memory_space=pltpu.SMEM)
    vmem = pl.BlockSpec(memory_space=pltpu.VMEM)
    return pl.pallas_call(
        route_kernel,
        in_specs=[smem, smem, vmem, vmem],
        out_specs=vmem,
        out_shape=jax.ShapeDtypeStruct((strips, length, c), BF),
        compiler_params=params(),
        name="route_strips",
    )(pick_row, rev, recv, own)


def corner_cell(a, b):
    return ((a + b) * 0.5).astype(BF).astype(F32)


def shifted(x, n, first, last):
    axis = x.ndim - 2
    sub = lax.broadcasted_iota(jnp.int32, first.shape, axis)
    down = pltpu.roll(x, 1, axis)
    up = pltpu.roll(x, n - 1, axis)
    head = jnp.where(sub == 0, first, lax.slice_in_dim(down, 0, 8, axis=axis))
    tail = jnp.where(sub == 7, last, lax.slice_in_dim(up, n - 8, n, axis=axis))
    down = jnp.concatenate([head, lax.slice_in_dim(down, 8, n, axis=axis)], axis=axis)
    up = jnp.concatenate([lax.slice_in_dim(up, 0, n - 8, axis=axis), tail], axis=axis)
    return down, up


def spread_columns(strip, n, sublane, buf):
    buf[pl.ds(sublane, n, 8), :] = strip
    return buf[...].reshape(n, 8, 128)


def cell8(cell):
    return jnp.broadcast_to(cell, (8, 128))


def padded_rows(x, halo, n, buf_l, buf_r):
    top, right, bottom, left = halo
    first = spread_columns(left, n, 0, buf_l)
    last = spread_columns(right, n, 7, buf_r)
    body_d, body_u = shifted(x, n, first, last)
    tl = corner_cell(top[0:1], left[0:1])
    tr = corner_cell(top[n - 1 : n], right[0:1])
    bl = corner_cell(bottom[0:1], left[n - 1 : n])
    br = corner_cell(bottom[n - 1 : n], right[n - 1 : n])
    top_d, top_u = shifted(top, n, cell8(tl), cell8(tr))
    bot_d, bot_u = shifted(bottom, n, cell8(bl), cell8(br))
    return (top_d, top, top_u), (body_d, x, body_u), (bot_d, bottom, bot_u)


def fill_pairs(y_ref, x, halo, n, buf_l, buf_r):
    half = n // 2
    top, body, bottom = padded_rows(x, halo, n, buf_l, buf_r)
    for s in range(3):
        b = body[s].astype(BF).reshape(half, 2, n, 128)
        y_ref[0, 0:n, s * 128 : s * 128 + 128] = top[s].astype(BF)
        y_ref[0:half, 0:n, 384 + s * 128 : 384 + s * 128 + 128] = b[:, 0]
        y_ref[1 : half + 1, 0:n, s * 128 : s * 128 + 128] = b[:, 1]
        y_ref[half, 0:n, 384 + s * 128 : 384 + s * 128 + 128] = bottom[s].astype(BF)


def fill_rows(u_ref, x, halo, n, buf_l, buf_r):
    top, body, bottom = padded_rows(x, halo, n, buf_l, buf_r)
    for s in range(3):
        lanes = slice(s * 128, s * 128 + 128)
        u_ref[0, 0:n, lanes] = top[s].astype(BF)
        u_ref[1 : n + 1, 0:n, lanes] = body[s].astype(BF)
        u_ref[n + 1, 0:n, lanes] = bottom[s].astype(BF)


def silu(s):
    return s / (1.0 + jnp.exp(-s))


def conv_pairs(y_ref, w_ref, q0, m, extra):
    n_p = y_ref.shape[1]
    a = y_ref[q0 : q0 + m].reshape(m * n_p, 768)
    b = y_ref[q0 + 1 : q0 + 1 + m].reshape(m * n_p, 768)
    acc = jnp.dot(a, w_ref[0:768, :], preferred_element_type=F32)
    acc = acc + jnp.dot(b, w_ref[768:1536, :], preferred_element_type=F32)
    acc = acc.reshape(m, n_p, 256)
    if extra is not None:
        acc = acc + extra
    return silu(acc)


def pair_chunks(n):
    half = n // 2
    m = 6 if half % 6 == 0 else half
    return [(q, m) for q in range(0, half, m)]


def emit_rims(y_ref, rims_ref, g, n, colbuf):
    def read(lo):
        return y_ref[g, :, :, lo : lo + 8, :].astype(F32).reshape(n, 8, 128)

    left, right = column_strips(read, n, colbuf)
    rims_ref[g, 0] = y_ref[g, 0, 0]
    rims_ref[g, 1] = right.astype(BF)
    rims_ref[g, 2] = y_ref[g, n // 2 - 1, 1]
    rims_ref[g, 3] = left.astype(BF)


def enc_kernel(x_ref, halo_ref, w_ref, y_ref, rims_ref, s_ref, pairs, buf_l, buf_r, colbuf, sumbuf):
    group, n = x_ref.shape[0], x_ref.shape[1]
    half = n // 2

    def one(g):
        halo = [halo_ref[g, e].astype(F32) for e in range(4)]
        fill_pairs(pairs, x_ref[g].astype(F32), halo, n, buf_l, buf_r)
        for q0, m in pair_chunks(n):
            out = conv_pairs(pairs, w_ref, q0, m, None).astype(BF)[:, 0:n]
            y_ref[g, q0 : q0 + m, 0] = out[:, :, 0:128]
            y_ref[g, q0 : q0 + m, 1] = out[:, :, 128:256]
            both = out[:, :, 0:128].astype(F32) + out[:, :, 128:256].astype(F32)
            sumbuf[...] = both.reshape(m * n, 128)
            small = sumbuf[pl.ds(0, m * half, 2), :] + sumbuf[pl.ds(1, m * half, 2), :]
            s_ref[g, q0 : q0 + m] = (small * 0.25).reshape(m, half, 128).astype(BF)
        emit_rims(y_ref, rims_ref, g, n, colbuf)

    for g in range(group):
        one(g)


def dec_kernel(
    x_ref, halo_ref, u_ref, uhalo_ref, w_ref, wu_ref, y_ref, rims_ref,
    pairs, rows, buf_l, buf_r, cbuf_l, cbuf_r, colbuf, acc_ref,
):
    group, n = x_ref.shape[0], x_ref.shape[1]
    half = n // 2
    hp = rows.shape[1]

    def one(g):
        halo = [halo_ref[g, e].astype(F32) for e in range(4)]
        uhalo = [uhalo_ref[g, e].astype(F32) for e in range(4)]
        fill_rows(rows, u_ref[g].astype(F32), uhalo, half, cbuf_l, cbuf_r)
        fill_pairs(pairs, x_ref[g].astype(F32), halo, n, buf_l, buf_r)
        for q0, m in pair_chunks(n):
            for b in range(2):
                acc = None
                for k in range(3):
                    lhs = rows[q0 + k : q0 + k + m, :, b * 128 : b * 128 + 256].reshape(m * hp, 256)
                    part = jnp.dot(lhs, wu_ref[b, k], preferred_element_type=F32)
                    acc = part if acc is None else acc + part
                acc = acc.reshape(m, hp, 256)
                for i in range(m):
                    for p in range(2):
                        acc_ref[p, i, pl.ds(b, half, 2), :] = acc[i, 0:half, p * 128 : p * 128 + 128]
            extra = jnp.concatenate([acc_ref[0], acc_ref[1]], axis=2)
            out = conv_pairs(pairs, w_ref, q0, m, extra).astype(BF)[:, 0:n]
            y_ref[g, q0 : q0 + m, 0] = out[:, :, 0:128]
            y_ref[g, q0 : q0 + m, 1] = out[:, :, 128:256]
        if rims_ref is not None:
            emit_rims(y_ref, rims_ref, g, n, colbuf)

    for g in range(group):
        one(g)


def group_of(tiles, want):
    return max(g for g in range(1, want + 1) if tiles % g == 0)


def pair_weights(w):
    zero = jnp.zeros((1,) + w.shape[1:], w.dtype)
    first = jnp.concatenate([w, zero], axis=0)
    second = jnp.concatenate([zero, w], axis=0)
    return jnp.concatenate([first.reshape(1536, 128), second.reshape(1536, 128)], axis=1)


def coarse_weights(w):
    w = w.astype(F32)
    zero = jnp.zeros_like(w[0])
    even = jnp.stack([w[0], w[1] + w[2], zero])
    odd = jnp.stack([zero, w[0] + w[1], w[2]])
    both = jnp.stack([even, odd], axis=3)
    left = jnp.stack([both[:, 0], both[:, 1] + both[:, 2]], axis=1)
    right = jnp.stack([both[:, 0] + both[:, 1], both[:, 2]], axis=1)
    return jnp.stack([left, right]).reshape(2, 3, 256, 256).astype(BF)


def tile_spec(group, *dims):
    return pl.BlockSpec((group,) + dims, lambda i: (i,) + (0,) * len(dims))


def whole_spec(shape):
    return pl.BlockSpec(shape, lambda i: (0,) * len(shape))


def enc_conv(x, halo, w, want):
    tiles, n, _, c = x.shape
    half, n_p = n // 2, up16(n)
    g = group_of(tiles, want)
    m = pair_chunks(n)[0][1]
    y, rims, s = pl.pallas_call(
        enc_kernel,
        grid=(tiles // g,),
        in_specs=[tile_spec(g, n, n, c), tile_spec(g, 4, n, c), whole_spec((1536, 256))],
        out_specs=[tile_spec(g, half, 2, n, c), tile_spec(g, 4, n, c), tile_spec(g, half, half, c)],
        out_shape=[
            jax.ShapeDtypeStruct((tiles, half, 2, n, c), BF),
            jax.ShapeDtypeStruct((tiles, 4, n, c), BF),
            jax.ShapeDtypeStruct((tiles, half, half, c), BF),
        ],
        scratch_shapes=[
            pltpu.VMEM((half + 1, n_p, 768), BF),
            pltpu.VMEM((n * 8, 128), F32),
            pltpu.VMEM((n * 8, 128), F32),
            pltpu.VMEM((n * 8, 128), F32),
            pltpu.VMEM((m * n, 128), F32),
        ],
        compiler_params=params(),
        cost_estimate=pl.CostEstimate(
            flops=tiles * n * n * 2 * 1536 * 128, bytes_accessed=tiles * n * n * 600, transcendentals=tiles * n * n * 128
        ),
        name="enc_conv",
    )(x, halo, pair_weights(w))
    return y.reshape(tiles, n, n, c), rims, s


def dec_conv(x, halo, u, uhalo, w, want, with_rims):
    tiles, n, _, c = x.shape
    half, n_p, h_p = n // 2, up16(n), up16(n // 2)
    g = group_of(tiles, want)
    m = pair_chunks(n)[0][1]
    kernel = dec_kernel if with_rims else (lambda *r: dec_kernel(*r[:7], None, *r[7:]))
    out = pl.pallas_call(
        kernel,
        grid=(tiles // g,),
        in_specs=[
            tile_spec(g, n, n, c), tile_spec(g, 4, n, c), tile_spec(g, half, half, c), tile_spec(g, 4, half, c),
            whole_spec((1536, 256)), whole_spec((2, 3, 256, 256)),
        ],
        out_specs=[tile_spec(g, half, 2, n, c)] + [tile_spec(g, 4, n, c)] * with_rims,
        out_shape=[jax.ShapeDtypeStruct((tiles, half, 2, n, c), BF)]
        + [jax.ShapeDtypeStruct((tiles, 4, n, c), BF)] * with_rims,
        scratch_shapes=[
            pltpu.VMEM((half + 1, n_p, 768), BF),
            pltpu.VMEM((half + 2, h_p, 384), BF),
            pltpu.VMEM((n * 8, 128), F32),
            pltpu.VMEM((n * 8, 128), F32),
            pltpu.VMEM((half * 8, 128), F32),
            pltpu.VMEM((half * 8, 128), F32),
            pltpu.VMEM((n * 8, 128), F32),
            pltpu.VMEM((2, m, n_p, 128), F32),
        ],
        compiler_params=params(),
        cost_estimate=pl.CostEstimate(
            flops=tiles * n * n * 2 * 2300 * 128, bytes_accessed=tiles * n * n * 600, transcendentals=tiles * n * n * 128
        ),
        name="dec_conv",
    )(x, halo, u, uhalo, pair_weights(w[:, :, c:]), coarse_weights(w[:, :, :c]))
    y = out[0].reshape(tiles, n, n, c)
    return (y, out[1]) if with_rims else y


def per_device(features, edge_table, w_enc0, w_enc1, w_enc2, w_mid, w_dec2, w_dec1, w_dec0):
    tiles = features.shape[0]
    devices = lax.axis_size("tile")
    position = lax.axis_index("tile")
    cap = pair_capacity(FACE_TILES, tiles)
    rows = devices * cap
    slot_row, pick_row, rev = routing_plan(edge_table, position, tiles, cap, devices)
    strip_count = tiles * 4
    buffer_rows = jnp.arange(rows, dtype=jnp.int32)
    send_map = (slot_row[None, :] == buffer_rows[:, None]).astype(BF)
    pick_columns = jnp.arange(rows + strip_count, dtype=jnp.int32)
    pick_map = (pick_row[:, None] == pick_columns[None, :]).astype(BF)

    def trade(strips):
        length = strips.shape[1]
        out = lax.all_to_all(
            strips.reshape(devices, cap * length, 128), "tile", split_axis=0, concat_axis=0, tiled=True
        )
        return out.reshape(rows, length, 128)

    def halo_big(rims):
        length = rims.shape[2]
        own = rims.reshape(strip_count, length, 128)
        recv = trade(pack_strips(slot_row, own, rows))
        return route_strips(pick_row, rev, recv, own).reshape(tiles, 4, length, 128)

    def halo_small(rims):
        length = rims.shape[2]
        flat = rims.reshape(strip_count, length * 128)
        outgoing = jnp.dot(send_map, flat, preferred_element_type=F32).astype(BF)
        incoming = trade(outgoing.reshape(rows, length, 128)).reshape(rows, length * 128)
        gathered = jnp.concatenate([incoming, flat], axis=0)
        halo = jnp.dot(pick_map, gathered, preferred_element_type=F32).astype(BF)
        halo = halo.reshape(strip_count, length, 128)
        halo = jnp.where(rev[:, None, None] == 1, halo[:, ::-1, :], halo)
        return halo.reshape(tiles, 4, length, 128)

    x0_rims = tile_rims(features)
    enc0, enc0_rims, x1 = enc_conv(features, halo_big(x0_rims), w_enc0, 1)
    x1_halo = halo_big(tile_rims(x1))
    enc0_halo = halo_big(enc0_rims)
    enc1, enc1_rims, x2 = enc_conv(x1, x1_halo, w_enc1, 4)
    x2_halo = halo_small(edge_rims(x2))
    enc1_halo = halo_big(enc1_rims)
    enc2 = conv_layer(assemble(x2, x2_halo), w_enc2)
    x3 = shrink(enc2)
    x3_halo = halo_small(edge_rims(x3))
    enc2_halo = halo_small(edge_rims(enc2))
    middle = conv_layer(assemble(x3, x3_halo), w_mid)
    mid_halo = halo_small(edge_rims(middle))
    upper = assemble(enlarge(middle), jnp.repeat(mid_halo, 2, axis=2))
    lower = assemble(enc2, enc2_halo)
    dec2 = conv_layer(jnp.concatenate([upper, lower], axis=3), w_dec2)
    dec2_halo = halo_small(edge_rims(dec2))
    dec1, dec1_rims = dec_conv(enc1, enc1_halo, dec2, dec2_halo, w_dec1, 4, True)
    dec1_halo = halo_big(dec1_rims)
    return dec_conv(enc0, enc0_halo, dec1, dec1_halo, w_dec0, 1, False)


def solution(mesh):
    return jax.shard_map(
        per_device,
        mesh=mesh,
        in_specs=(P(("grp", "tile"), None, None, None), P(), P(), P(), P(), P(), P(), P(), P()),
        out_specs=P(("grp", "tile"), None, None, None),
        check_vma=False,
    )
```

time: 611 us -> 463 us (0.76)
  Pallas kernels: 0 us -> 165 us
  matrix products: 175 us -> 19.1 us
  waiting for transfers between devices: 215 us -> 125 us
  local copies, waits for them, and re-layouts: 137 us -> 66.4 us
    pallas_call x0 -> x16, Pallas kernels: none -> 165 us  [the longest x2 66.4 us: dec_conv(): pl.pallas_call(kernel, grid=(tiles // g,), in_specs=[tile_spec(g, n, n, c...]
    conv_general_dilated x7 -> x3, matrix products: 151 us -> 8.79 us  [conv_layer(): lax.conv_general_dilated(padded, weight, (1, 1), 'VALID', dimension_numbe...]
    all_to_all x10, waiting for transfers between devices: 215 us -> 125 us  [trade(): lax.all_to_all(strips.reshape(devices, cap * length, 128), 'tile', split_...]
    reshape x28 -> x6, local copies, waits for them, and re-layouts: 34.5 us -> 4.38 us  [the longest x5 4.32 us: halo_small(): halo = halo.reshape(strip_count, length, 128)]
    another operation x0 -> x27, local copies, waits for them, and re-layouts: none -> 27.9 us  [the longest x5 7.77 us: halo_small(): trade(outgoing.reshape(rows, length, 128)).reshape(rows, length * 128)]
    unnamed x131 -> x109, local copies, waits for them, and re-layouts: 40.3 us -> 16.2 us
    convert_element_type x1 -> x12, local copies, waits for them, and re-layouts: 14 us -> 0.05 us  [corner(): ((one_side.astype(F32) + other_side.astype(F32)) * 0.5).astype(field.dtype)]
    dot_general x20 -> x10, matrix products: 24.2 us -> 10.3 us  [the longest x5 8.29 us: halo_small(): halo = jnp.dot(pick_map, gathered, preferred_element_type=F32).astype(BF)]
  transfers between devices with their start and end apart: 10 -> 10, of which waited for: 10 -> 10; matrix products, arithmetic and copies ran while one was open for 18% -> 15% of each run, Pallas kernels for 0% -> 8%
where the time goes in v1:
time: 463 us; the launch traced here: 455 us
  Pallas kernels  165 us (36%)
  waiting for transfers between devices  125 us (27%)
  local copies, waits for them, and re-layouts  66.4 us (14%)
  starting transfers between devices  53.1 us (11%)
  other arithmetic  25.4 us (5%)
  matrix products  19.1 us (4%)
    all_to_all x10, waiting for transfers between devices, trade(): lax.all_to_all(strips.reshape(devices, cap * length, 128), 'tile', split_...  125 us
    pallas_call x2, Pallas kernels, dec_conv(): pl.pallas_call(kernel, grid=(tiles // g,), in_specs=[tile_spec(g, n, n, c...  66.4 us
    pallas_call x2, Pallas kernels, enc_conv(): pl.pallas_call(enc_kernel, grid=(tiles // g,), in_specs=[tile_spec(g, n,...  53.5 us
    all_to_all x10, starting transfers between devices, trade(): lax.all_to_all(strips.reshape(devices, cap * length, 128), 'tile', split_...  53.1 us
    pallas_call x5, Pallas kernels, route_strips(): pl.pallas_call(route_kernel, in_specs=[smem, smem, vmem, vmem], out_specs...  18.6 us
    unnamed x109, local copies, waits for them, and re-layouts  16.2 us
    pallas_call x2, Pallas kernels, tile_rims(): pl.pallas_call(rims_kernel, grid=(tiles,), in_specs=[pl.BlockSpec((1, n,...  14.7 us
    pallas_call x5, Pallas kernels, pack_strips(): pl.pallas_call(pack_kernel, in_specs=[pl.BlockSpec(memory_space=pltpu.SME...  11.6 us
  transfers between devices with their start and end apart: 10, of which 10 were waited for; matrix products, arithmetic and copies ran while one was open for 15% of the time, Pallas kernels for 8%

profile of v1, /device:TPU:15, one launch (start us, length us, event | category | flops | bytes accessed | tf_op | source)
XLA Modules:
  0.0 455.4 jit_solution(13257366965262535439)
XLA Ops:
  2.1 3.9 gather_fusion
  7.1 13.9 %tile_rims.2 = bf16[24,4,48,128]{3,2,1,0:T(8,128)(2,1)S(1)} custom-call(bf16[24,48,48,128]{3,2,1,0:T(8,128)(2,1)} %x_ref.3), custom_call_target="tpu_custom_call" | custom-call | tf_op jit(solution)/shard_map/tile_rims/pallas_call | solution.py:174
  21.0 1.9 pack_strips.5
  22.9 1.3 copy-done.2
  24.2 6.7 %all-to-all-start = ((bf16[16,528,128]{2,1,0:T(8,128)(2,1)}), bf16[16,528,128]{2,1,0:T(8,128)(2,1)}, u32[]{:S(2)}, u32[]{:S(2)}) async-start(bf16[16,528,128]{2,1,0:T(8,128)(2,1)} %bitcast.262), calls=%async_computation | async-start | bytes 4325376 | tf_op jit(solution)/shard_map/all_to_all | solution.py:515
  32.3 47.6 %all-to-all-done = bf16[16,528,128]{2,1,0:T(8,128)(2,1)} async-done(((bf16[16,528,128]{2,1,0:T(8,128)(2,1)}), bf16[16,528,128]{2,1,0:T(8,128)(2,1)}, u32[]{:S(2)}, u32[]{:S(2)}) %all-to-all-start) | async-done | bytes 2162720 | tf_op jit(solution)/shard_map/all_to_all | solution.py:515
  79.8 4.4 route_strips.5
  84.3 39.9 %enc_conv.2 = (bf16[24,24,2,48,128]{4,3,2,1,0:T(8,128)(2,1)}, bf16[24,4,48,128]{3,2,1,0:T(8,128)(2,1)S(1)}, bf16[24,24,24,128]{3,2,1,0:T(8,128)(2,1)}) custom-call(bf16[24,48,48,128]{3,2,1,0:T(8,128)(2,1)} %x_ref.3, bf16[24,4,48,128]{3,2,1,0:T(8,128)(2,1)S(1)} %bitcast.277, bf16[1536,256]{1,0:T(8,128)(2,1)S(1)} %pad_maximum_fusion.5.w_ref), custom_call_target="tpu_custom_call" | custom-call | flops 21743271936 | bytes 33177600 | tf_op jit(solution)/shard_map/enc_conv/pallas_call | solution.py:438
  124.2 2.0 copy-done.5
  126.9 1.8 pack_strips.7
  129.8 4.9 %all-to-all-start.2 = ((bf16[16,264,128]{2,1,0:T(8,128)(2,1)}), bf16[16,264,128]{2,1,0:T(8,128)(2,1)S(1)}, u32[]{:S(2)}, u32[]{:S(2)}) async-start(bf16[16,264,128]{2,1,0:T(8,128)(2,1)} %bitcast.271), calls=%async_computation.2 | async-start | bytes 2162688 | tf_op jit(solution)/shard_map/all_to_all | solution.py:515
  134.7 2.1 pad_maximum_fusion.6.w_ref
  136.8 23.5 %all-to-all-done.2 = bf16[16,264,128]{2,1,0:T(8,128)(2,1)S(1)} async-done(((bf16[16,264,128]{2,1,0:T(8,128)(2,1)}), bf16[16,264,128]{2,1,0:T(8,128)(2,1)S(1)}, u32[]{:S(2)}, u32[]{:S(2)}) %all-to-all-start.2) | async-done | bytes 1081376 | tf_op jit(solution)/shard_map/all_to_all | solution.py:515
  160.3 3.3 route_strips.7
  163.6 13.6 %enc_conv.3 = (bf16[24,12,2,24,128]{4,3,2,1,0:T(8,128)(2,1)}, bf16[24,4,24,128]{3,2,1,0:T(8,128)(2,1)S(1)}, bf16[24,12,12,128]{3,2,1,0:T(8,128)(2,1)S(1)}) custom-call(bf16[24,24,24,128]{3,2,1,0:T(8,128)(2,1)} %get-tuple-element.15.x_ref, bf16[24,4,24,128]{3,2,1,0:T(8,128)(2,1)S(1)} %bitcast.280, bf16[1536,256]{1,0:T(8,128)(2,1)S(1)} %copy-done.12), custom_call_target="tpu_custom_call" | custom-call | flops 5435817984 | bytes 8294400 | tf_op jit(solution)/shard_map/enc_conv/pallas_call | solution.py:438
  179.7 2.5 reshape_reshape.30
  182.2 5.2 %all-to-all-start.4 = ((bf16[16,132,128]{2,1,0:T(8,128)(2,1)}), bf16[16,132,128]{2,1,0:T(8,128)(2,1)}, u32[]{:S(2)}, u32[]{:S(2)}) async-start(bf16[16,132,128]{2,1,0:T(8,128)(2,1)} %reshape_reshape.30), calls=%async_computation.4 | async-start | bytes 1114112 | tf_op jit(solution)/shard_map/all_to_all | solution.py:515
  188.6 2.9 pack_strips.8
  191.5 10.2 %all-to-all-done.4 = bf16[16,132,128]{2,1,0:T(8,128)(2,1)} async-done(((bf16[16,132,128]{2,1,0:T(8,128)(2,1)}), bf16[16,132,128]{2,1,0:T(8,128)(2,1)}, u32[]{:S(2)}, u32[]{:S(2)}) %all-to-all-start.4) | async-done | bytes 540704 | tf_op jit(solution)/shard_map/all_to_all | solution.py:515
  201.6 2.5 reshape_reshape.31
  204.1 2.3 convolution_convert_fusion.5
  206.4 1.9 reshape.337
  208.3 2.0 rev.15
  210.3 1.3 broadcast_select_fusion.2
  213.6 2.5 multiply_convert_fusion
  219.6 4.9 %all-to-all-start.5 = ((bf16[16,66,128]{2,1,0:T(8,128)(2,1)}), bf16[16,66,128]{2,1,0:T(8,128)(2,1)S(1)}, u32[]{:S(2)}, u32[]{:S(2)}) async-start(bf16[16,66,128]{2,1,0:T(8,128)(2,1)} %reshape_reshape.32), calls=%async_computation.5 | async-start | bytes 589824 | tf_op jit(solution)/shard_map/all_to_all | solution.py:515
  226.0 1.5 reshape_reshape.36
  227.5 5.7 %all-to-all-done.5 = bf16[16,66,128]{2,1,0:T(8,128)(2,1)S(1)} async-done(((bf16[16,66,128]{2,1,0:T(8,128)(2,1)}), bf16[16,66,128]{2,1,0:T(8,128)(2,1)S(1)}, u32[]{:S(2)}, u32[]{:S(2)}) %all-to-all-start.5) | async-done | bytes 270368 | tf_op jit(solution)/shard_map/all_to_all | solution.py:515
  233.2 5.4 %all-to-all-start.7 = ((bf16[16,132,128]{2,1,0:T(8,128)(2,1)}), bf16[16,132,128]{2,1,0:T(8,128)(2,1)S(1)}, u32[]{:S(2)}, u32[]{:S(2)}) async-start(bf16[16,132,128]{2,1,0:T(8,128)(2,1)} %reshape_reshape.36), calls=%async_computation.7 | async-start | bytes 1114112 | tf_op jit(solution)/shard_map/all_to_all | solution.py:515
  241.5 1.7 multiply_convert_fusion.1
  245.9 7.1 %all-to-all-done.7 = bf16[16,132,128]{2,1,0:T(8,128)(2,1)S(1)} async-done(((bf16[16,132,128]{2,1,0:T(8,128)(2,1)}), bf16[16,132,128]{2,1,0:T(8,128)(2,1)S(1)}, u32[]{:S(2)}, u32[]{:S(2)}) %all-to-all-start.7) | async-done | bytes 540704 | tf_op jit(solution)/shard_map/all_to_all | solution.py:515
  253.0 5.3 %all-to-all-start.6 = ((bf16[16,66,128]{2,1,0:T(8,128)(2,1)}), bf16[16,66,128]{2,1,0:T(8,128)(2,1)}, u32[]{:S(2)}, u32[]{:S(2)}) async-start(bf16[16,66,128]{2,1,0:T(8,128)(2,1)} %reshape_reshape.34), calls=%async_computation.6 | async-start | bytes 589824 | tf_op jit(solution)/shard_map/all_to_all | solution.py:515
  258.3 1.4 reshape_reshape.37
  259.7 1.4 convolution_convert_fusion.4
  265.5 1.4 all-to-all-done.6
  266.9 5.5 %all-to-all-start.3 = ((bf16[16,264,128]{2,1,0:T(8,128)(2,1)}), bf16[16,264,128]{2,1,0:T(8,128)(2,1)S(1)}, u32[]{:S(2)}, u32[]{:S(2)}) async-start(bf16[16,264,128]{2,1,0:T(8,128)(2,1)} %bitcast.28), calls=%async_computation.3 | async-start | bytes 2162688 | tf_op jit(solution)/shard_map/all_to_all | solution.py:515
  272.4 1.9 reshape_reshape.35
  274.3 2.0 convolution_convert_fusion.8
  276.3 1.8 reshape.345
  278.1 1.7 rev.17
  282.4 4.6 %fusion = f32[24,12,12,128]{3,0,2,1:T(8,128)S(1)} fusion(bf16[3,3,256,128]{3,2,1,0:T(8,128)(2,1)S(1)} %copy-done, bf16[24,1,14,128]{3,0,2,1:T(8,128)(2,1)S(1)} %copy-done.34, bf16[24,12,1,128]{3,0,2,1:T(8,128)(2,1)S(1)} %bitcast.343, bf16[24,12,12,128]{3,0,2,1:T(8,128)(2,1)S(1)} %copy-done.16, bf16[24,12,1,128]{3,0,2,1:T(8,128)(2,1)S(1)} %bitcast.342, ...), kind=kOutput, calls=%fused_computation.6 | convolution fusion | flops 2062516224 | bytes 4767744 | tf_op jit(solution)/shard_map/conv_general_dilated | solution.py:126
  289.9 1.5 reshape_reshape.38
  291.4 6.7 %all-to-all-done.3 = bf16[16,264,128]{2,1,0:T(8,128)(2,1)S(1)} async-done(((bf16[16,264,128]{2,1,0:T(8,128)(2,1)}), bf16[16,264,128]{2,1,0:T(8,128)(2,1)S(1)}, u32[]{:S(2)}, u32[]{:S(2)}) %all-to-all-start.3) | async-done | bytes 1081376 | tf_op jit(solution)/shard_map/all_to_all | solution.py:515
  298.1 4.8 %all-to-all-start.8 = ((bf16[16,132,128]{2,1,0:T(8,128)(2,1)}), bf16[16,132,128]{2,1,0:T(8,128)(2,1)S(1)}, u32[]{:S(2)}, u32[]{:S(2)}) async-start(bf16[16,132,128]{2,1,0:T(8,128)(2,1)} %reshape_reshape.38), calls=%async_computation.8 | async-start | bytes 1114112 | tf_op jit(solution)/shard_map/all_to_all | solution.py:515
  302.9 3.2 pack_strips.6
  306.1 11.1 %all-to-all-done.8 = bf16[16,132,128]{2,1,0:T(8,128)(2,1)S(1)} async-done(((bf16[16,132,128]{2,1,0:T(8,128)(2,1)}), bf16[16,132,128]{2,1,0:T(8,128)(2,1)S(1)}, u32[]{:S(2)}, u32[]{:S(2)}) %all-to-all-start.8) | async-done | bytes 540704 | tf_op jit(solution)/shard_map/all_to_all | solution.py:515
  318.0 5.4 %all-to-all-start.1 = ((bf16[16,528,128]{2,1,0:T(8,128)(2,1)}), bf16[16,528,128]{2,1,0:T(8,128)(2,1)}, u32[]{:S(2)}, u32[]{:S(2)}) async-start(bf16[16,528,128]{2,1,0:T(8,128)(2,1)} %bitcast.17), calls=%async_computation.1 | async-start | bytes 4325376 | tf_op jit(solution)/shard_map/all_to_all | solution.py:515
  323.4 1.9 slice_convert_fusion.1
  329.6 2.0 stack.98
  334.9 2.0 pad_maximum_fusion.8.wu_ref
  336.9 2.3 fusion.153
  340.2 3.3 route_strips.8
  343.5 1.7 reshape_reshape.39
  345.2 1.4 convolution_convert_fusion.3
  348.8 18.7 %dec_conv.2 = (bf16[24,12,2,24,128]{4,3,2,1,0:T(8,128)(2,1)}, bf16[24,4,24,128]{3,2,1,0:T(8,128)(2,1)S(1)}) custom-call(bf16[24,24,24,128]{3,2,1,0:T(8,128)(2,1)} %bitcast.361, bf16[24,4,24,128]{3,2,1,0:T(8,128)(2,1)S(1)} %bitcast.278, bf16[24,12,12,128]{3,2,1,0:T(8,128)(2,1)} %copy-done.13, bf16[24,4,12,128]{3,2,1,0:T(8,128)(2,1)S(1)} %bitcast.281, ...), custom_call_target="tpu_custom_call" | custom-call | flops 8139571200 | bytes 8294400 | tf_op jit(solution)/shard_map/dec_conv/pallas_call | solution.py:470
  367.4 1.8 pack_strips.9
  370.3 1.9 all-to-all-done.1
  372.2 5.0 %all-to-all-start.9 = ((bf16[16,264,128]{2,1,0:T(8,128)(2,1)}), bf16[16,264,128]{2,1,0:T(8,128)(2,1)S(1)}, u32[]{:S(2)}, u32[]{:S(2)}) async-start(bf16[16,264,128]{2,1,0:T(8,128)(2,1)} %bitcast.269), calls=%async_computation.9 | async-start | bytes 2162688 | tf_op jit(solution)/shard_map/all_to_all | solution.py:515
  379.4 2.0 stack.110
  384.9 2.0 pad_maximum_fusion.10.r_5_
  387.9 4.4 route_strips.6
  393.3 9.5 %all-to-all-done.9 = bf16[16,264,128]{2,1,0:T(8,128)(2,1)S(1)} async-done(((bf16[16,264,128]{2,1,0:T(8,128)(2,1)}), bf16[16,264,128]{2,1,0:T(8,128)(2,1)S(1)}, u32[]{:S(2)}, u32[]{:S(2)}) %all-to-all-start.9) | async-done | bytes 1081376 | tf_op jit(solution)/shard_map/all_to_all | solution.py:515
  402.9 3.3 route_strips.9
  407.3 47.7 %dec_conv.3 = bf16[24,24,2,48,128]{4,3,2,1,0:T(8,128)(2,1)} custom-call(bf16[24,48,48,128]{3,2,1,0:T(8,128)(2,1)} %bitcast.360, bf16[24,4,48,128]{3,2,1,0:T(8,128)(2,1)S(1)} %bitcast.276, bf16[24,24,24,128]{3,2,1,0:T(8,128)(2,1)} %bitcast.362, bf16[24,4,24,128]{3,2,1,0:T(8,128)(2,1)S(1)} %bitcast.279, bf16[1536,256]{1,0:T(8,128)(2,1)S(1)} %copy-done.11, ...), custom_call_target="tpu_custom_call" | custom-call | flops 32558284800 | bytes 33177600 | tf_op jit(solution)/shard_map/dec_conv/pallas_call | solution.py:470
  (243 shorter events, 52.6 us)
Async XLA Ops:
  0.0 281.8 %copy-start = (bf16[3,3,256,128]{3,2,1,0:T(8,128)(2,1)S(1)}, bf16[3,3,256,128]{3,2,1,0:T(8,128)(2,1)}, u32[]{:S(2)}) copy-start(bf16[3,3,256,128]{3,2,1,0:T(8,128)(2,1)} %param.15) | copy-start | bytes 1769476
  1.8 4.7 %copy-start.38 = (s32[96,1]{0,1:T(1,128)}, s32[96,1]{0,1:T(1,128)S(1)}, u32[]{:S(2)}) copy-start(s32[96,1]{0,1:T(1,128)S(1)} %get-tuple-element.130) | copy-start | bytes 1156
  1.8 4.8 %copy-start.39 = (s32[96,1]{0,1:T(1,128)}, s32[96,1]{0,1:T(1,128)S(1)}, u32[]{:S(2)}) copy-start(s32[96,1]{0,1:T(1,128)S(1)} %get-tuple-element.26) | copy-start | bytes 1156
  6.6 0.5 copy-start.37
  22.9 1.3 copy-start.2
  24.2 6.7 %copy-start.31 = (bf16[3,3,128,128]{3,2,1,0:T(8,128)(2,1)S(1)}, bf16[3,3,128,128]{3,2,1,0:T(8,128)(2,1)}, u32[]{:S(2)}) copy-start(bf16[3,3,128,128]{3,2,1,0:T(8,128)(2,1)} %param.12) | copy-start | bytes 884740
  24.2 6.7 %copy-start.32 = (bf16[3,3,128,128]{3,2,1,0:T(8,128)(2,1)S(1)}, bf16[3,3,128,128]{3,2,1,0:T(8,128)(2,1)}, u32[]{:S(2)}) copy-start(bf16[3,3,128,128]{3,2,1,0:T(8,128)(2,1)} %param.11) | copy-start | bytes 884740
  24.2 55.6 %all-to-all-start = ((bf16[16,528,128]{2,1,0:T(8,128)(2,1)}), bf16[16,528,128]{2,1,0:T(8,128)(2,1)}, u32[]{:S(2)}, u32[]{:S(2)}) async-start(bf16[16,528,128]{2,1,0:T(8,128)(2,1)} %bitcast.262), calls=%async_computation | async-start | bytes 4325376 | tf_op jit(solution)/shard_map/all_to_all | solution.py:515
  124.2 2.0 copy-start.5
  128.8 1.0 copy-start.4
  129.8 30.6 %all-to-all-start.2 = ((bf16[16,264,128]{2,1,0:T(8,128)(2,1)}), bf16[16,264,128]{2,1,0:T(8,128)(2,1)S(1)}, u32[]{:S(2)}, u32[]{:S(2)}) async-start(bf16[16,264,128]{2,1,0:T(8,128)(2,1)} %bitcast.271), calls=%async_computation.2 | async-start | bytes 2162688 | tf_op jit(solution)/shard_map/all_to_all | solution.py:515
  160.3 3.3 copy-start.12
  177.9 0.7 copy-start.22
  182.2 19.5 %all-to-all-start.4 = ((bf16[16,132,128]{2,1,0:T(8,128)(2,1)}), bf16[16,132,128]{2,1,0:T(8,128)(2,1)}, u32[]{:S(2)}, u32[]{:S(2)}) async-start(bf16[16,132,128]{2,1,0:T(8,128)(2,1)} %reshape_reshape.30), calls=%async_computation.4 | async-start | bytes 1114112 | tf_op jit(solution)/shard_map/all_to_all | solution.py:515
  212.6 1.0 copy-start.42
  216.1 8.5 %copy-start.15 = (bf16[24,12,12,128]{3,0,2,1:T(8,128)(2,1)}, bf16[24,12,12,128]{3,0,2,1:T(8,128)(2,1)S(1)}, u32[]{:S(2)}) copy-start(bf16[24,12,12,128]{3,0,2,1:T(8,128)(2,1)S(1)} %multiply_convert_fusion) | copy-start | bytes 2654212
  217.0 0.7 copy-start.27
  217.8 0.7 copy-start.29
  219.6 13.6 %all-to-all-start.5 = ((bf16[16,66,128]{2,1,0:T(8,128)(2,1)}), bf16[16,66,128]{2,1,0:T(8,128)(2,1)S(1)}, u32[]{:S(2)}, u32[]{:S(2)}) async-start(bf16[16,66,128]{2,1,0:T(8,128)(2,1)} %reshape_reshape.32), calls=%async_computation.5 | async-start | bytes 589824 | tf_op jit(solution)/shard_map/all_to_all | solution.py:515
  225.7 7.5 %copy-start.19 = (bf16[12,8,12,128]{3,1,2,0:T(8,128)(2,1)}, bf16[12,8,12,128]{3,1,2,0:T(8,128)(2,1)S(1)}, u32[]{:S(2)}) copy-start(bf16[12,8,12,128]{3,1,2,0:T(8,128)(2,1)S(1)} %copy.401) | copy-start | bytes 884740
  233.2 19.8 %all-to-all-start.7 = ((bf16[16,132,128]{2,1,0:T(8,128)(2,1)}), bf16[16,132,128]{2,1,0:T(8,128)(2,1)S(1)}, u32[]{:S(2)}, u32[]{:S(2)}) async-start(bf16[16,132,128]{2,1,0:T(8,128)(2,1)} %reshape_reshape.36), calls=%async_computation.7 | async-start | bytes 1114112 | tf_op jit(solution)/shard_map/all_to_all | solution.py:515
  240.5 1.0 copy-start.43
  243.2 0.7 copy-start.25
  243.9 15.8 %copy-start.20 = (bf16[12,8,12,128]{3,1,2,0:T(8,128)(2,1)S(1)}, bf16[12,8,12,128]{3,1,2,0:T(8,128)(2,1)}, u32[]{:S(2)}) copy-start(bf16[12,8,12,128]{3,1,2,0:T(8,128)(2,1)} %copy-done.19) | copy-start | bytes 884740
  243.9 15.8 %copy-start.40 = (s32[96]{0:T(128)S(1)}, s32[96]{0:T(128)}, u32[]{:S(2)}) copy-start(s32[96]{0:T(128)} %fusion.134) | copy-start | bytes 1156
  244.0 0.7 copy-start.28
  253.0 13.9 %all-to-all-start.6 = ((bf16[16,66,128]{2,1,0:T(8,128)(2,1)}), bf16[16,66,128]{2,1,0:T(8,128)(2,1)}, u32[]{:S(2)}, u32[]{:S(2)}) async-start(bf16[16,66,128]{2,1,0:T(8,128)(2,1)} %reshape_reshape.34), calls=%async_computation.6 | async-start | bytes 589824 | tf_op jit(solution)/shard_map/all_to_all | solution.py:515
  264.1 10.2 %copy-start.41 = (s32[96]{0:T(128)S(1)}, s32[96]{0:T(128)}, u32[]{:S(2)}) copy-start(s32[96]{0:T(128)} %fusion.134) | copy-start | bytes 1156
  266.9 31.2 %all-to-all-start.3 = ((bf16[16,264,128]{2,1,0:T(8,128)(2,1)}), bf16[16,264,128]{2,1,0:T(8,128)(2,1)S(1)}, u32[]{:S(2)}, u32[]{:S(2)}) async-start(bf16[16,264,128]{2,1,0:T(8,128)(2,1)} %bitcast.28), calls=%async_computation.3 | async-start | bytes 2162688 | tf_op jit(solution)/shard_map/all_to_all | solution.py:515
  279.8 1.8 copy-start.26
  281.2 1.2 copy-start.16
  281.2 1.2 copy-start.33
  281.2 1.2 copy-start.34
  281.2 1.2 copy-start.35
  281.3 1.2 copy-start.36
  287.6 1.1 copy-start.13
  288.9 0.7 copy-start.21
  298.1 19.2 %all-to-all-start.8 = ((bf16[16,132,128]{2,1,0:T(8,128)(2,1)}), bf16[16,132,128]{2,1,0:T(8,128)(2,1)S(1)}, u32[]{:S(2)}, u32[]{:S(2)}) async-start(bf16[16,132,128]{2,1,0:T(8,128)(2,1)} %reshape_reshape.38), calls=%async_computation.8 | async-start | bytes 1114112 | tf_op jit(solution)/shard_map/all_to_all | solution.py:515
  317.2 0.8 copy-start.14
  318.0 54.2 %all-to-all-start.1 = ((bf16[16,528,128]{2,1,0:T(8,128)(2,1)}), bf16[16,528,128]{2,1,0:T(8,128)(2,1)}, u32[]{:S(2)}, u32[]{:S(2)}) async-start(bf16[16,528,128]{2,1,0:T(8,128)(2,1)} %bitcast.17), calls=%async_computation.1 | async-start | bytes 4325376 | tf_op jit(solution)/shard_map/all_to_all | solution.py:515
  323.4 2.0 copy-start.30
  328.4 3.2 copy-start.24
  345.2 2.5 copy-start.8
  347.6 1.1 copy-start.9
  369.3 1.0 copy-start.3
  372.2 9.3 %copy-start.23 = (bf16[3,1,128,2,128]{4,2,1,0,3:T(8,128)(2,1)S(1)}, bf16[3,1,128,2,128]{4,2,1,0,3:T(8,128)(2,1)}, u32[]{:S(2)}) copy-start(bf16[3,1,128,2,128]{4,2,1,0,3:T(8,128)(2,1)} %get-tuple-element.138) | copy-start | bytes 589828
  372.2 30.7 %all-to-all-start.9 = ((bf16[16,264,128]{2,1,0:T(8,128)(2,1)}), bf16[16,264,128]{2,1,0:T(8,128)(2,1)S(1)}, u32[]{:S(2)}, u32[]{:S(2)}) async-start(bf16[16,264,128]{2,1,0:T(8,128)(2,1)} %bitcast.269), calls=%async_computation.9 | async-start | bytes 2162688 | tf_op jit(solution)/shard_map/all_to_all | solution.py:515
  384.8 2.1 copy-start.17
  384.9 2.1 copy-start.18
  392.3 1.0 copy-start.6
  402.9 3.3 copy-start.7
  402.9 3.3 copy-start.10
  406.2 1.1 copy-start.11
  407.3 47.7 %copy-start.1 = (bf16[3,3,256,128]{3,2,1,0:T(8,128)(2,1)S(1)}, bf16[3,3,256,128]{3,2,1,0:T(8,128)(2,1)}, u32[]{:S(2)}) copy-start(bf16[3,3,256,128]{3,2,1,0:T(8,128)(2,1)} %param.15) | copy-start | bytes 1769476
